TPU v7x, 32 devices: a whole 2x2x4 slice. The times are simulated.
32 devices in a mesh: rows: 8 (over z, x), seq: 4 (over y, core).
Axes of the slice: x: 2, y: 2, z: 4, core: 2. Of those that a mesh axis runs over, the one named last changes fastest.
Arguments:
- frames_in: bfloat16 [16, 4096, 512], P('rows', 'seq'), may hold values from -6 to 6
- lengths: int32 [16, 4], P('rows'), may hold values from 1 to 2048, 4096 in all within a row
- bw_ids: int32 [16, 4], P('rows'), may hold values from 0 to 3
- owner_list: int32 [137], replicated, may hold values from 0 to 7, as said below
- master: float32 [216, 32, 512], P('rows')
- moment1: float32 [216, 32, 512], P('rows')
- moment2: float32 [216, 32, 512], P('rows'), as said below
- wave_grad: bfloat16 [16, 1310720], P('rows', 'seq'), may hold values from -6 to 6
Outputs:
- waveform: float32 [16, 1310720], P('rows', 'seq')
- input_grad: float32 [16, 4096, 512], P('rows', 'seq')
- new_master: float32 [216, 32, 512], P('rows')
- new_moment1: float32 [216, 32, 512], P('rows')
- new_moment2: float32 [216, 32, 512], P('rows')
Inputs may be any that keep to these rules, and one draw needn't show every extreme that they name: `owner_list`: no index along rows owns more than 27 buckets, and some index owns exactly 27. `moment2`: every entry is positive.
All inputs are finite; a program needn't handle non-finite values.
Results may differ from a plain program's by a relative error of at most 0.012.
The roundings to bfloat16 on the way count: a program that leaves them out, or rounds other values in their place, can miss the bound.
Values may be sent and summed in bfloat16 or wider, within the bound.
No kernel may reach another device: no remote copies, remote signals or barrier semaphores. Data moves between devices by JAX's collectives and lax.ppermute only.
A program may use at most 192 MiB of HBM per device.

v0:
```python
import math
import jax
import jax.numpy as jnp
from jax import lax
from jax.sharding import PartitionSpec as P

FF = 1536
NFFT = 1280
HOP = 320
NBW = 4
KW = 7
UTT = 4
BR = 32
STEP_COUNT = 6
BINS = 641
NOUT = 1282
VROWS = 20
IN_ROWS = 3
HEAD_ROWS = 3
PR = 4380
NB = 137
NORM_EPS = 1e-06
ENV_FLOOR = 0.5
BETA_ONE = 0.8
BETA_TWO = 0.9
LEARN_RATE = 0.04
WEIGHT_DECAY = 0.01
ADAM_EPS = 1e-08


def padded(block, sides, width):
    for axis, dim in sides:
        count = lax.axis_size(axis)
        forward = [(i, i + 1) for i in range(count - 1)]
        backward = [(target, source) for source, target in forward]
        low = lax.ppermute(
            lax.slice_in_dim(block, block.shape[dim] - width, None, axis=dim), axis, forward
        )
        high = lax.ppermute(lax.slice_in_dim(block, 0, width, axis=dim), axis, backward)
        block = jnp.concatenate([low, block, high], axis=dim)
    return block


def from_behind(block, axis, distance):
    devices = range(lax.axis_size(axis))
    route = [(i - distance, i) for i in devices if i - distance in devices]
    return lax.ppermute(block, axis, route)


def slot_maps(owner_list, owner_count, slot_count):
    bucket_count = owner_list.shape[0]
    bucket_index = jnp.arange(bucket_count, dtype=jnp.int32)
    same_owner = owner_list[None, :] == owner_list[:, None]
    before = bucket_index[None, :] < bucket_index[:, None]
    slot_rank = jnp.sum((same_owner & before).astype(jnp.int32), axis=1)
    bucket_place = owner_list * slot_count + slot_rank
    targets = jnp.arange(owner_count * slot_count, dtype=jnp.int32)
    slot_match = bucket_place[None, :] == targets[:, None]
    found_bucket = jnp.sum(slot_match.astype(jnp.int32) * bucket_index[None, :], axis=1)
    source = jnp.where(jnp.any(slot_match, axis=1), found_bucket, bucket_count)
    return (bucket_place, source)


def synthesis_table():
    bin_index = jnp.arange(BINS, dtype=jnp.int32)[:, None]
    tap_index = jnp.arange(NFFT, dtype=jnp.int32)[None, :]
    turns = bin_index * tap_index % NFFT
    angle = turns.astype(jnp.float32) * (2.0 * math.pi / NFFT)
    edge_bin = (bin_index == 0) | (bin_index == NFFT // 2)
    factor = jnp.where(edge_bin, 1.0, 2.0).astype(jnp.float32) / NFFT
    return jnp.concatenate([factor * jnp.cos(angle), -factor * jnp.sin(angle)], axis=0)


def hann_window():
    angle = jnp.arange(NFFT, dtype=jnp.int32).astype(jnp.float32) * (2.0 * math.pi / NFFT)
    return 0.5 - 0.5 * jnp.cos(angle)


def segment_ids(lengths, first_index, span):
    starts = jnp.cumsum(lengths, axis=1) - lengths
    frame_index = first_index + jnp.arange(span, dtype=jnp.int32)
    return jnp.sum((starts[:, None, :] <= frame_index[None, :, None]).astype(jnp.int32), axis=2) - 1


def layer_norm(values):
    row_mean = jnp.mean(values, axis=-1, keepdims=True)
    centered = values - row_mean
    return centered * lax.rsqrt(jnp.mean(centered * centered, axis=-1, keepdims=True) + NORM_EPS)


def ada_norm(values, scale_rows, shift_rows):
    return layer_norm(values) * scale_rows + shift_rows


def final_norm(values, norm_gain, norm_bias):
    return layer_norm(values) * norm_gain[None, :] + norm_bias[None, :]


def exact_gelu(values):
    return jax.nn.gelu(values, approximate=False)


def contract(left_side, right_side, left_dim, right_dim):
    return lax.dot_general(
        left_side,
        right_side,
        (((left_dim,), (right_dim,)), ((), ())),
        preferred_element_type=jnp.float32,
    )


def local(frames_in, lengths, bw_ids, owner_list, master, moment1, moment2, wave_grad):
    rows_here, frames_here, channels = frames_in.shape
    slot_count = master.shape[0]
    frame_count = rows_here * frames_here
    lap_count = NFFT // HOP
    rim_width = (KW - 1) // 2
    margin = max(rim_width, lap_count - 1)
    bucket_place, source = slot_maps(owner_list, lax.axis_size("rows"), slot_count)
    gathered = lax.all_gather(master.astype(jnp.bfloat16), "rows", axis=0, tiled=True)
    buckets = jnp.take(gathered, bucket_place, axis=0)
    weight_table = buckets.reshape(-1, channels)[:PR]
    w_in = weight_table[:FF]
    w_out = weight_table[FF : 2 * FF]
    w_head = weight_table[2 * FF : 2 * FF + NOUT]
    row_start = 2 * FF + NOUT
    channel_rows = weight_table[row_start : row_start + VROWS].astype(jnp.float32)
    row_start = row_start + VROWS
    bias_in = weight_table[row_start : row_start + IN_ROWS].reshape(-1).astype(jnp.float32)
    row_start = row_start + IN_ROWS
    bias_head = (
        weight_table[row_start : row_start + HEAD_ROWS].reshape(-1)[:NOUT].astype(jnp.float32)
    )
    conv_weight = channel_rows[:KW]
    conv_bias = channel_rows[KW]
    ada_scale = channel_rows[KW + 1 : KW + 1 + NBW]
    ada_shift = channel_rows[KW + 1 + NBW : KW + 1 + 2 * NBW]
    vec_base = KW + 1 + 2 * NBW
    bias_out = channel_rows[vec_base]
    layer_scale = channel_rows[vec_base + 1]
    norm_gain = channel_rows[vec_base + 2]
    norm_bias = channel_rows[vec_base + 3]
    first_index = lax.axis_index("seq") * frames_here - margin
    segment = segment_ids(lengths, first_index, frames_here + 2 * margin)
    own_segment = segment[:, margin : margin + frames_here]
    halo_frames = padded(frames_in, (("seq", 1),), rim_width)
    wide_frames = halo_frames.astype(jnp.float32)
    conv_keep = []
    conv_out = jnp.zeros((rows_here, frames_here, channels), jnp.float32) + conv_bias
    for tap_index in range(KW):
        lower = margin - rim_width + tap_index
        keep = (segment[:, lower : lower + frames_here] == own_segment).astype(jnp.float32)[
            :, :, None
        ]
        conv_keep.append(keep)
        conv_out = (
            conv_out
            + keep * wide_frames[:, tap_index : tap_index + frames_here] * conv_weight[tap_index]
        )
    conv_out = conv_out.reshape(frame_count, channels)
    utt_pick = (own_segment[:, :, None] == jnp.arange(UTT, dtype=jnp.int32)[None, None, :]).astype(
        jnp.int32
    )
    frame_ids = jnp.sum(utt_pick * bw_ids[:, None, :], axis=2).reshape(frame_count)
    bw_onehot = (frame_ids[:, None] == jnp.arange(NBW, dtype=jnp.int32)[None, :]).astype(
        jnp.float32
    )
    scale_rows = jnp.dot(bw_onehot, ada_scale, precision=lax.Precision.HIGHEST)
    shift_rows = jnp.dot(bw_onehot, ada_shift, precision=lax.Precision.HIGHEST)
    ada_value, ada_back = jax.vjp(ada_norm, conv_out, scale_rows, shift_rows)
    ada_low = ada_value.astype(jnp.bfloat16)
    hidden_pre = contract(ada_low, w_in, 1, 1) + bias_in[None, :]
    act_value, gelu_back = jax.vjp(exact_gelu, hidden_pre)
    act_low = act_value.astype(jnp.bfloat16)
    branch = contract(act_low, w_out, 1, 0) + bias_out[None, :]
    frames_flat = frames_in.reshape(frame_count, channels).astype(jnp.float32)
    residual = frames_flat + layer_scale[None, :] * branch
    normed_value, final_back = jax.vjp(final_norm, residual, norm_gain, norm_bias)
    normed_low = normed_value.astype(jnp.bfloat16)
    head_out = contract(normed_low, w_head, 1, 1) + bias_head[None, :]
    magnitude = jnp.exp(head_out[:, :BINS])
    phase_angle = head_out[:, BINS:]
    real_part = magnitude * jnp.cos(phase_angle)
    imag_part = magnitude * jnp.sin(phase_angle)
    spectrum_low = jnp.concatenate([real_part, imag_part], axis=1).astype(jnp.bfloat16)
    synthesis = synthesis_table().astype(jnp.bfloat16)
    signal = contract(spectrum_low, synthesis, 1, 0)
    window_rows = hann_window().reshape(lap_count, HOP)
    pieces = signal.reshape(rows_here, frames_here, lap_count, HOP) * window_rows[None, None, :, :]
    lap_keep = []
    numerator = jnp.zeros((rows_here, frames_here + lap_count - 1, HOP), jnp.float32)
    envelope = jnp.zeros((rows_here, frames_here, HOP), jnp.float32)
    for lap_index in range(lap_count):
        ahead = margin + lap_index
        keep = (segment[:, ahead : ahead + frames_here] == own_segment).astype(jnp.float32)[
            :, :, None
        ]
        lap_keep.append(keep)
        numerator = numerator + jnp.pad(
            keep * pieces[:, :, lap_index], ((0, 0), (lap_index, lap_count - 1 - lap_index), (0, 0))
        )
        behind = margin - lap_index
        back_keep = (segment[:, behind : behind + frames_here] == own_segment).astype(jnp.float32)[
            :, :, None
        ]
        envelope = envelope + back_keep * (window_rows[lap_index] ** 2)[None, None, :]
    arrived = from_behind(numerator[:, frames_here:], "seq", 1)
    numerator = numerator[:, :frames_here] + jnp.pad(
        arrived, ((0, 0), (0, frames_here - lap_count + 1), (0, 0))
    )
    denominator = jnp.maximum(envelope, ENV_FLOOR)
    waveform = (numerator / denominator).reshape(rows_here, frames_here * HOP)
    scaled = wave_grad.astype(jnp.float32).reshape(rows_here, frames_here, HOP) / denominator
    later_rows = from_behind(scaled[:, : lap_count - 1], "seq", -1)
    reach_rows = jnp.concatenate([scaled, later_rows], axis=1)
    signal_grad = jnp.stack(
        [
            lap_keep[lap_index]
            * window_rows[lap_index][None, None, :]
            * reach_rows[:, lap_index : lap_index + frames_here]
            for lap_index in range(lap_count)
        ],
        axis=2,
    )
    signal_low = signal_grad.reshape(frame_count, NFFT).astype(jnp.bfloat16)
    spec_grad = contract(signal_low, synthesis, 1, 1)
    real_grad = spec_grad[:, :BINS]
    imag_grad = spec_grad[:, BINS:]
    head_grad = jnp.concatenate(
        [
            real_grad * real_part + imag_grad * imag_part,
            imag_grad * real_part - real_grad * imag_part,
        ],
        axis=1,
    ).astype(jnp.bfloat16)
    grad_w_head = contract(head_grad, normed_low, 0, 0)
    grad_b_head = jnp.sum(head_grad, axis=0, dtype=jnp.float32)
    normed_grad = contract(head_grad, w_head, 1, 0)
    residual_grad, grad_gain, grad_bias = final_back(normed_grad)
    branch_low = (layer_scale[None, :] * residual_grad).astype(jnp.bfloat16)
    grad_layer_scale = jnp.sum(residual_grad * branch, axis=0)
    grad_w_out = contract(act_low, branch_low, 0, 0)
    grad_b_out = jnp.sum(branch_low, axis=0, dtype=jnp.float32)
    act_grad = contract(branch_low, w_out, 1, 1)
    pre_low = gelu_back(act_grad)[0].astype(jnp.bfloat16)
    grad_w_in = contract(pre_low, ada_low, 0, 0)
    grad_b_in = jnp.sum(pre_low, axis=0, dtype=jnp.float32)
    ada_grad = contract(pre_low, w_in, 1, 0)
    conv_grad, scale_grad_rows, shift_grad_rows = ada_back(ada_grad)
    grad_scales = lax.dot_general(
        bw_onehot, scale_grad_rows, (((0,), (0,)), ((), ())), precision=lax.Precision.HIGHEST
    )
    grad_shifts = lax.dot_general(
        bw_onehot, shift_grad_rows, (((0,), (0,)), ((), ())), precision=lax.Precision.HIGHEST
    )
    conv_rows = conv_grad.reshape(rows_here, frames_here, channels)
    grad_conv_b = jnp.sum(conv_grad, axis=0)
    grad_conv_w = jnp.stack(
        [
            jnp.sum(
                conv_keep[tap_index]
                * conv_rows
                * wide_frames[:, tap_index : tap_index + frames_here],
                axis=(0, 1),
            )
            for tap_index in range(KW)
        ],
        axis=0,
    )
    halo_grad = padded(conv_rows, (("seq", 1),), rim_width)
    input_grad = residual_grad.reshape(rows_here, frames_here, channels)
    for tap_index in range(KW):
        lower = margin + rim_width - tap_index
        keep = (segment[:, lower : lower + frames_here] == own_segment).astype(jnp.float32)[
            :, :, None
        ]
        begin = 2 * rim_width - tap_index
        input_grad = (
            input_grad + conv_weight[tap_index] * keep * halo_grad[:, begin : begin + frames_here]
        )
    vec_grads = jnp.concatenate(
        [
            grad_conv_w,
            grad_conv_b[None, :],
            grad_scales,
            grad_shifts,
            jnp.stack([grad_b_out, grad_layer_scale, grad_gain, grad_bias], axis=0),
        ],
        axis=0,
    )
    in_rows = grad_b_in.reshape(IN_ROWS, channels)
    head_rows = jnp.pad(grad_b_head, (0, HEAD_ROWS * channels - NOUT)).reshape(HEAD_ROWS, channels)
    grad_table = jnp.concatenate(
        [grad_w_in, grad_w_out, grad_w_head, vec_grads, in_rows, head_rows], axis=0
    )
    grad_buckets = jnp.pad(grad_table, ((0, NB * BR - PR), (0, 0))).reshape(NB, BR, channels)
    empty_bucket = jnp.zeros((1, BR, channels), jnp.float32)
    summed = lax.psum(grad_buckets, ("rows", "seq"))
    extended = jnp.concatenate([summed, empty_bucket], axis=0)
    my_sources = lax.dynamic_slice_in_dim(source, lax.axis_index("rows") * slot_count, slot_count)
    reduced = jnp.take(extended, my_sources, axis=0)
    first_new = BETA_ONE * moment1 + (1.0 - BETA_ONE) * reduced
    second_new = BETA_TWO * moment2 + (1.0 - BETA_TWO) * reduced * reduced
    first_fix = 1.0 - BETA_ONE**STEP_COUNT
    second_fix = 1.0 - BETA_TWO**STEP_COUNT
    master_new = master - LEARN_RATE * (
        first_new / first_fix / (jnp.sqrt(second_new / second_fix) + ADAM_EPS)
        + WEIGHT_DECAY * master
    )
    return (waveform, input_grad, master_new, first_new, second_new)


def solution(mesh):
    in_specs = (
        P("rows", "seq", None),
        P("rows", None),
        P("rows", None),
        P(),
        P("rows", None, None),
        P("rows", None, None),
        P("rows", None, None),
        P("rows", "seq"),
    )
    out_specs = (
        P("rows", "seq"),
        P("rows", "seq", None),
        P("rows", None, None),
        P("rows", None, None),
        P("rows", None, None),
    )
    return jax.shard_map(local, mesh=mesh, in_specs=in_specs, out_specs=out_specs, check_vma=False)
```

profile of v0, /device:TPU:0, one launch (start us, length us, event | category | flops | bytes accessed | tf_op | source)
XLA Modules:
  0.0 546.3 jit_solution(15566940357598605938)
XLA Ops:
  7.2 2.5 convert_element_type.160
  10.6 2.4 collective-permute-start
  12.9 1.3 collective-permute-start.1
  15.8 2.7 reshape.271
  18.5 2.2 copy.39
  21.1 2.9 fusion.48
  24.8 1.3 collective-permute-start.3
  26.2 2.7 reshape.270
  28.9 2.2 copy.37
  33.0 2.8 fusion.47
  35.9 15.2 %multiply_convert_fusion.2 = (bf16[641,1280]{1,0:T(8,128)(2,1)}, bf16[641,1280]{1,0:T(8,128)(2,1)}) fusion(f32[641]{0:T(1024)S(1)} %fusion.74, f32[641]{0:T(1024)S(1)} %select_multiply_fusion), kind=kLoop, calls=%fused_computation.89 | loop fusion | flops 10666240 | bytes 3287048 | tf_op jit(solution)/shard_map/convert.12
  51.9 9.4 %concatenate.35 = bf16[2,1030,512]{2,1,0:T(8,128)(2,1)S(1)} concatenate(bf16[2,3,512]{2,1,0:T(4,128)(2,1)S(1)} %collective-permute-done, bf16[2,1024,512]{2,1,0:T(8,128)(2,1)} %param.8, bf16[2,3,512]{2,1,0:T(4,128)(2,1)S(1)} %collective-permute-done.1), dimensions={1} | concatenate | bytes 4218880 | tf_op jit(solution)/shard_map/concatenate | solution.py:40
  61.3 2.6 convert_element_type.164
  63.8 4.7 fusion.55
  68.5 3.2 pad_maximum_fusion.1
  71.7 10.2 %copy.40 = bf16[2,1024,4,320]{1,0,3,2:T(2,128)(2,1)} copy(bf16[2,1024,4,320]{1,3,0,2:T(8,128)(2,1)} %pad_maximum_fusion.1) | data formatting | bytes 10485760 | tf_op jit(solution)/shard_map/stack | solution.py:216
  81.9 4.8 copy.45
  86.7 9.7 %fusion.49 = f32[2048,1282]{0,1:T(8,128)} fusion(bf16[2048,1280]{0,1:T(8,128)(2,1)S(1)} %bitcast.122, bf16[641,1280]{1,0:T(8,128)(2,1)S(1)} %copy-done.20, bf16[641,1280]{1,0:T(8,128)(2,1)S(1)} %copy-done.21), kind=kOutput, calls=%fused_computation.122 | convolution fusion | flops 6727936000 | bytes 19026944 | tf_op jit(solution)/shard_map/dot_general | solution.py:104
  96.5 25.9 %all-gather.2.cloned.1.call-done = bf16[216,32,512]{2,1,0:T(8,128)(2,1)} async-done(((bf16[27,32,512]{2,1,0:T(8,128)(2,1)}), bf16[216,32,512]{2,1,0:T(8,128)(2,1)}) %all-gather.2.cloned.1.call-update) | async-done | bytes 7077904 | tf_op jit(solution)/shard_map/all_gather | solution.py:120
  122.3 10.9 %gather_fusion = bf16[137,32,512]{2,1,0:T(8,128)(2,1)} fusion(bf16[216,32,512]{2,1,0:T(8,128)(2,1)} %all-gather.2.cloned.1.call-done, s32[1024]{0:T(1024)S(1)} %pad_clamp_fusion.1), kind=kCustom, calls=%fused_computation | custom fusion | bytes 8978980 | tf_op jit(solution)/shard_map/jit(_take)/gather | solution.py:121
  133.3 4.1 bitcast_select_fusion
  137.5 2.6 broadcast_select_fusion
  140.2 2.4 slice-done
  142.7 6.1 %fusion.88 = (f32[2,1024]{1,0:T(2,128)S(1)}, f32[2,1024,512]{2,1,0:T(8,128)S(1)}) fusion(f32[512]{0:T(512)S(1)} %bitcast.134, f32[2,1030,512]{2,1,0:T(8,128)S(1)} %bitcast.114, f32[2,1024]{1,0:T(2,128)S(1)} %get-tuple-element.69, f32[512]{0:T(512)S(1)} %bitcast.136, f32[2,1024]{1,0:T(2,128)S(1)} %get-tuple-element.70, f32[512]{0:T(512)S(1)} %bitcast.138, ...), kind=kLoop, calls=%fused_computation.211 | loop fusion | flops 22018048 | bytes 33628160 | tf_op jit(solution)/shard_map/jvp()/reduce_sum | solution.py:86
  149.7 2.4 bitcast_subtract_fusion
  152.1 2.5 fusion.60
  154.7 2.3 fusion.89
  157.8 4.0 add_convert_fusion.3
  161.8 31.4 %multiply_convert_fusion = (bf16[2048,1536]{1,0:T(8,128)(2,1)S(1)}, f32[2048,1536]{1,0:T(8,128)}, f32[2048,1536]{1,0:T(8,128)}) fusion(f32[1536]{0:T(1024)S(1)} %reshape.280, bf16[2048,512]{1,0:T(8,128)(2,1)S(1)} %add_convert_fusion.3, bf16[1536,512]{1,0:T(8,128)(2,1)S(1)} %bitcast.123), kind=kOutput, calls=%fused_computation.6 | convolution fusion | flops 3428843520 | bytes 35133440 | tf_op jit(solution)/shard_map/dot_general | solution.py:104
  193.2 5.6 %fusion.86 = (f32[2048]{0:T(1024)S(1)}, f32[2048,512]{1,0:T(8,128)S(1)}, f32[2048,512]{1,0:T(8,128)}) fusion(f32[512]{0:T(512)S(1)} %bitcast.159, f32[512]{0:T(512)S(1)} %bitcast.157, bf16[2,1024,512]{2,1,0:T(8,128)(2,1)S(1)} %copy-done.16, bf16[2048,1536]{1,0:T(8,128)(2,1)S(1)} %get-tuple-element.32, bf16[1536,512]{1,0:T(8,128)(2,1)S(1)} %bitcast.125), kind=kOutput, calls=%fused_computation.210 | convolution fusion | flops 3226466304 | bytes 18362368 | tf_op jit(solution)/shard_map/dot_general | solution.py:104
  198.8 1.9 copy-done.8
  201.6 5.8 %convolution_add_fusion = f32[2048,1282]{0,1:T(8,128)S(1)} fusion(f32[1282]{0:T(1024)S(1)} %slice_convert_fusion.1, bf16[4384,512]{1,0:T(8,128)(2,1)} %copy-done.13, f32[2048,512]{1,0:T(8,128)} %copy-done.8, f32[512]{0:T(512)S(1)} %bitcast.169, f32[512]{0:T(512)S(1)} %bitcast.163, f32[2048]{0:T(1024)S(1)} %fusion.70, f32[2048]{0:T(1024)S(1)} %broadcast_multiply_fusion), kind=kOutput, calls=%fused_computation.22 | convolution fusion | flops 2696417280 | bytes 16040968 | tf_op jit(solution)/shard_map/dot_general | solution.py:104
  207.5 24.2 %add_convert_fusion.1 = (bf16[2048,641]{0,1:T(8,128)(2,1)S(1)}, bf16[2048,641]{0,1:T(8,128)(2,1)S(1)}, bf16[2048,641]{0,1:T(8,128)(2,1)}, bf16[2048,641]{0,1:T(8,128)(2,1)}) fusion(f32[2048,1282]{0,1:T(8,128)} %fusion.49, f32[2048,1282]{0,1:T(8,128)S(1)} %convolution_add_fusion), kind=kLoop, calls=%fused_computation.31 | loop fusion | flops 15753216 | bytes 31506432 | tf_op jit(solution)/shard_map/convert.2
  231.7 1.3 convert_reduce_fusion.1
  233.9 6.2 %multiply_reduce_fusion = (f32[512]{0:T(512)S(1)}, f32[2048]{0:T(1024)S(1)}, f32[512]{0:T(512)S(1)}, f32[2048,512]{1,0:T(8,128)S(1)}) fusion(f32[2048,512]{1,0:T(8,128)S(1)} %copy-done.9, f32[2048]{0:T(1024)S(1)} %fusion.70, f32[2048]{0:T(1024)S(1)} %broadcast_multiply_fusion, f32[512]{0:T(512)S(1)} %bitcast.164, bf16[4384,512]{1,0:T(8,128)(2,1)} %copy-done.13, ...), kind=kOutput, calls=%fused_computation.64 | convolution fusion | flops 2707436544 | bytes 14989312 | tf_op jit(solution)/shard_map/dot_general | solution.py:104
  240.1 4.6 fusion.52
  244.7 2.0 fusion.85
  249.5 3.6 fusion.95
  253.1 16.6 %convert_reduce_fusion = (f32[1536]{0:T(1024)S(1)}, bf16[2048,1536]{1,0:T(8,128)(2,1)}) fusion(f32[2048,1536]{1,0:T(8,128)} %get-tuple-element.33, bf16[2048,512]{1,0:T(8,128)(2,1)} %copy-done.19, bf16[1536,512]{1,0:T(8,128)(2,1)} %bitcast.126, f32[2048,1536]{1,0:T(8,128)} %get-tuple-element.84, f32[1536]{0:T(1024)S(1)} %reshape.280), kind=kOutput, calls=%fused_computation.4 | convolution fusion | flops 3274701312 | bytes 35139584 | tf_op jit(solution)/shard_map/dot_general | solution.py:104
  269.7 6.7 %multiply_reduce_fusion.9 = (f32[2048]{0:T(1024)S(1)}, f32[2048,512]{1,0:T(8,128)S(1)}) fusion(f32[2048,512]{1,0:T(8,128)S(1)} %copy-done.4, f32[2048,512]{1,0:T(8,128)S(1)} %copy-done.6, bf16[2048,1536]{1,0:T(8,128)(2,1)} %get-tuple-element.90, bf16[1536,512]{1,0:T(8,128)(2,1)} %bitcast.124), kind=kOutput, calls=%fused_computation.76 | convolution fusion | flops 3224369152 | bytes 20455424 | tf_op jit(solution)/shard_map/dot_general | solution.py:104
  276.4 5.1 fusion.94
  281.5 2.2 fusion.27
  283.7 1.7 fusion.59
  285.5 5.5 %fusion.84 = (f32[2048]{0:T(1024)S(1)}, f32[2048,512]{1,0:T(8,128)S(1)}) fusion(f32[2048]{0:T(1024)S(1)} %fusion.69, f32[2048]{0:T(1024)S(1)} %copy-done.39, f32[2048,512]{1,0:T(8,128)} %copy-done.7, f32[2048,512]{1,0:T(8,128)} %fusion.60, f32[2048]{0:T(1024)S(1)} %bitcast.132, f32[2,1024,512]{2,1,0:T(8,128)} %copy-done), kind=kLoop, calls=%fused_computation.208 | loop fusion | flops 7337984 | bytes 16809984 | tf_op jit(solution)/shard_map/transpose(jvp())/reduce_sum | solution.py:87
  291.5 3.2 slice-done.2
  294.7 5.3 multiply_reduce_fusion.2
  300.1 27.2 %concatenate.42 = f32[4380,512]{1,0:T(8,128)} concatenate(f32[1536,512]{1,0:T(8,128)} %fusion.94, f32[1536,512]{1,0:T(8,128)S(1)} %fusion.95, f32[1282,512]{1,0:T(8,128)} %fusion.52, f32[1,512]{1,0:T(1,128)S(1)} %bitcast.156, f32[1,512]{1,0:T(1,128)S(1)} %bitcast.155, f32[1,512]{1,0:T(1,128)S(1)} %bitcast.154, f32[1,512]{1,0:T(1,128)S(1)} %bitcast.153, f32[1,512]{1,0:T(1,128)S(1)} %bitcast.152, ...), dimensions={0} | concatenate | bytes 17940480 | tf_op jit(solution)/shard_map/concatenate | solution.py:293
  327.2 8.1 %pad.35 = f32[4384,512]{1,0:T(8,128)} pad(f32[4380,512]{1,0:T(8,128)} %concatenate.42, f32[]{:T(128)} %constant.72.clone.1), padding=0_4x0_0 | pad | bytes 17948676 | tf_op jit(solution)/shard_map/jit(_pad)/pad | solution.py:296
  335.3 1.7 copy-done.15
  337.1 13.9 %fusion.6 = f32[2048,1280]{0,1:T(8,128)} fusion(bf16[2048,641]{0,1:T(8,128)(2,1)} %get-tuple-element.41, bf16[2048,641]{0,1:T(8,128)(2,1)S(1)} %copy-done.15, bf16[641,1280]{1,0:T(8,128)(2,1)} %get-tuple-element.91, bf16[641,1280]{1,0:T(8,128)(2,1)} %get-tuple-element.92), kind=kOutput, calls=%fused_computation.34 | convolution fusion | flops 6738438144 | bytes 19018752 | tf_op jit(solution)/shard_map/dot_general | solution.py:104
  350.9 14.4 %reshape.268 = f32[2,1024,4,320]{1,0,3,2:T(2,128)} reshape(f32[2048,1280]{0,1:T(8,128)} %fusion.6) | data formatting | bytes 20971520 | tf_op jit(solution)/shard_map/reshape | solution.py:189
  365.4 8.5 %copy_multiply_fusion = f32[2,1024,4,320]{1,3,0,2:T(8,128)S(1)} fusion(f32[2,1024,4,320]{1,0,3,2:T(2,128)} %reshape.268, f32[4,320]{1,0:T(4,128)S(1)} %copy-done.52), kind=kLoop, calls=%fused_computation.21 | loop fusion | flops 2621440 | bytes 20976640 | tf_op jit(solution)/shard_map/mul | solution.py:189
  374.2 1.8 fusion.46
  376.4 1.5 collective-permute-start.2
  377.9 2.3 pad_add_fusion
  382.3 4.4 collective-permute-start.5
  386.8 2.4 fusion.43
  389.2 2.6 copy.36
  391.9 4.1 reshape.269
  396.1 20.3 %fusion.13 = f32[2,1024,512]{2,1,0:T(8,128)} fusion(f32[2,3,512]{2,1,0:T(4,128)S(1)} %collective-permute-done.5, f32[2,3,512]{2,1,0:T(4,128)S(1)} %collective-permute-done.4, f32[2,1024,512]{2,1,0:T(8,128)} %bitcast.119, f32[2,1024,512]{2,1,0:T(8,128)} %bitcast.118, f32[512]{0:T(512)S(1)} %bitcast.135, f32[2,1024]{1,0:T(2,128)S(1)} %copy-done.31, ...), kind=kLoop, calls=%fused_computation.46 | loop fusion | flops 27262976 | bytes 12670976 | tf_op jit(solution)/shard_map/add | solution.py:279
  416.3 103.8 %all-reduce.10.cloned.1.call-done = f32[137,32,512]{2,1,0:T(8,128)} async-done(((f32[137,32,512]{2,1,0:T(8,128)}), f32[137,32,512]{2,1,0:T(8,128)}) %all-reduce.10.cloned.1.call-update) | async-done | bytes 8978448 | tf_op jit(solution)/shard_map/psum | solution.py:298
  520.2 9.1 %concatenate.43 = f32[138,32,512]{2,1,0:T(8,128)} pad(f32[137,32,512]{2,1,0:T(8,128)} %all-reduce.10.cloned.1.call-done, f32[]{:T(128)} %constant.72.clone.1), padding=0_1x0_0x0_0 | pad | bytes 18022404 | tf_op jit(solution)/shard_map/concatenate | solution.py:299
  529.3 4.5 gather_fusion.1
  533.8 5.5 %multiply_subtract_fusion = (f32[27,32,512]{2,1,0:T(8,128)}, f32[27,32,512]{2,1,0:T(8,128)}, f32[27,32,512]{2,1,0:T(8,128)}) fusion(f32[27,32,512]{2,1,0:T(8,128)S(1)} %copy-done.12, f32[27,32,512]{2,1,0:T(8,128)S(1)} %gather_fusion.1, pred[27]{0:T(512)(128)(4,1)S(1)} %copy-done.68, f32[27,32,512]{2,1,0:T(8,128)} %param.13, f32[27,32,512]{2,1,0:T(8,128)} %param.14), kind=kLoop, calls=%fused_computation.127 | loop fusion | flops 7077888 | bytes 12386331 | tf_op jit(solution)/shard_map/sub | solution.py:306
  (220 shorter events, 16.0 us)
Async XLA Ops:
  7.2 115.2 %all-gather.2.cloned.1.call-start = ((), (), s32[]{:S(2)}) async-start(), calls=%async_computation | async-start | bytes 7962624 | tf_op jit(solution)/shard_map/all_gather | solution.py:120
  9.8 510.4 %all-reduce.10.cloned.1.call-start = ((), (), s32[]{:S(2)}) async-start(), calls=%async_computation.1 | async-start | bytes 17956864 | tf_op jit(solution)/shard_map/psum | solution.py:298
  10.6 41.3 %collective-permute-start = (bf16[2,3,512]{2,1,0:T(4,128)(2,1)S(1)}, bf16[2,3,512]{2,1,0:T(4,128)(2,1)S(1)}, u32[]{:S(2)}, u32[]{:S(2)}) collective-permute-start(bf16[2,3,512]{2,1,0:T(4,128)(2,1)S(1)} %get-tuple-element.55), channel_id=1, source_target_pairs={{0,1},{1,2},{2,3},{4,5},{5,6},{6,7},{8,9},{9,10},{10,11},{12,13},{... | collective-permute-start | bytes 18440 | tf_op jit(solution)/shard_map/ppermute | solution.py:36
  12.9 38.9 %collective-permute-start.1 = (bf16[2,3,512]{2,1,0:T(4,128)(2,1)S(1)}, bf16[2,3,512]{2,1,0:T(4,128)(2,1)S(1)}, u32[]{:S(2)}, u32[]{:S(2)}) collective-permute-start(bf16[2,3,512]{2,1,0:T(4,128)(2,1)S(1)} %get-tuple-element.54), channel_id=1, source_target_pairs={{1,0},{2,1},{3,2},{5,4},{6,5},{7,6},{9,8},{10,9},{11,10},{13,12},{... | collective-permute-start | bytes 18440 | tf_op jit(solution)/shard_map/ppermute | solution.py:39
  20.9 12.1 %copy-start.44 = (f32[320]{0:T(512)}, f32[320]{0:T(512)S(1)}, u32[]{:S(2)}) copy-start(f32[320]{0:T(512)S(1)} %get-tuple-element.75) | copy-start | bytes 3844
  20.9 12.1 %copy-start.46 = (f32[320]{0:T(512)}, f32[320]{0:T(512)S(1)}, u32[]{:S(2)}) copy-start(f32[320]{0:T(512)S(1)} %get-tuple-element.76) | copy-start | bytes 3844
  20.9 12.1 %copy-start.48 = (f32[320]{0:T(512)}, f32[320]{0:T(512)S(1)}, u32[]{:S(2)}) copy-start(f32[320]{0:T(512)S(1)} %get-tuple-element.77) | copy-start | bytes 3844
  20.9 12.1 %copy-start.50 = (f32[320]{0:T(512)}, f32[320]{0:T(512)S(1)}, u32[]{:S(2)}) copy-start(f32[320]{0:T(512)S(1)} %get-tuple-element.78) | copy-start | bytes 3844
  21.1 119.1 %copy-start.24 = (f32[2,1024]{1,0:T(2,128)}, f32[2,1024]{1,0:T(2,128)S(1)}, u32[]{:S(2)}) copy-start(f32[2,1024]{1,0:T(2,128)S(1)} %get-tuple-element.68) | copy-start | bytes 24580
  21.1 119.1 %copy-start.26 = (f32[2,1024]{1,0:T(2,128)}, f32[2,1024]{1,0:T(2,128)S(1)}, u32[]{:S(2)}) copy-start(f32[2,1024]{1,0:T(2,128)S(1)} %get-tuple-element.72) | copy-start | bytes 24580
  21.1 119.1 %copy-start.28 = (f32[2,1024]{1,0:T(2,128)}, f32[2,1024]{1,0:T(2,128)S(1)}, u32[]{:S(2)}) copy-start(f32[2,1024]{1,0:T(2,128)S(1)} %get-tuple-element.73) | copy-start | bytes 24580
  21.1 119.1 %copy-start.30 = (f32[2,1024]{1,0:T(2,128)}, f32[2,1024]{1,0:T(2,128)S(1)}, u32[]{:S(2)}) copy-start(f32[2,1024]{1,0:T(2,128)S(1)} %get-tuple-element.69) | copy-start | bytes 24580
  21.1 119.1 %copy-start.32 = (f32[2,1024]{1,0:T(2,128)}, f32[2,1024]{1,0:T(2,128)S(1)}, u32[]{:S(2)}) copy-start(f32[2,1024]{1,0:T(2,128)S(1)} %get-tuple-element.70) | copy-start | bytes 24580
  21.1 119.1 %copy-start.34 = (f32[2,1024]{1,0:T(2,128)}, f32[2,1024]{1,0:T(2,128)S(1)}, u32[]{:S(2)}) copy-start(f32[2,1024]{1,0:T(2,128)S(1)} %get-tuple-element.71) | copy-start | bytes 24580
  24.8 39.0 %collective-permute-start.3 = (f32[2,3,320]{1,2,0:T(8,128)}, f32[2,3,320]{1,2,0:T(8,128)}, u32[]{:S(2)}, u32[]{:S(2)}) collective-permute-start(f32[2,3,320]{1,2,0:T(8,128)} %slice.387), channel_id=1, source_target_pairs={{1,0},{2,1},{3,2},{5,4},{6,5},{7,6},{9,8},{10,9},{11,10},{13,12},{... | collective-permute-start | bytes 23048 | tf_op jit(solution)/shard_map/ppermute | solution.py:47
  26.2 4.9 copy-start.67
  26.2 6.7 %copy-start.69 = (s32[2,4]{1,0:T(2,128)S(1)}, s32[2,4]{1,0:T(2,128)}, u32[]{:S(2)}) copy-start(s32[2,4]{1,0:T(2,128)} %param.10) | copy-start | bytes 100
  51.8 105.1 %copy-start.36 = (s32[1,8,2,128]{3,1,2,0:T(8,128)}, s32[1,8,2,128]{3,1,2,0:T(8,128)S(1)}, u32[]{:S(2)}) copy-start(s32[1,8,2,128]{3,1,2,0:T(8,128)S(1)} %copy.53) | copy-start | bytes 24580
  81.9 4.8 copy-start.20
  81.9 4.8 copy-start.21
  133.3 4.2 copy-start.1
  137.4 14.7 %copy-start.13 = (bf16[4384,512]{1,0:T(8,128)(2,1)}, bf16[4384,512]{1,0:T(8,128)(2,1)S(1)}, u32[]{:S(2)}) copy-start(bf16[4384,512]{1,0:T(8,128)(2,1)S(1)} %bitcast_select_fusion) | copy-start | bytes 13467652
  137.4 5.3 slice-start
  137.5 5.2 slice-start.1
  140.1 8.7 %copy-start.53 = (f32[1,512]{1,0:T(1,128)}, f32[1,512]{1,0:T(1,128)S(1)}, u32[]{:S(2)}) copy-start(f32[1,512]{1,0:T(1,128)S(1)} %get-tuple-element.59) | copy-start | bytes 6148
  140.1 8.7 %copy-start.55 = (f32[1,512]{1,0:T(1,128)}, f32[1,512]{1,0:T(1,128)S(1)}, u32[]{:S(2)}) copy-start(f32[1,512]{1,0:T(1,128)S(1)} %get-tuple-element.60) | copy-start | bytes 6148
  140.1 8.7 %copy-start.57 = (f32[1,512]{1,0:T(1,128)}, f32[1,512]{1,0:T(1,128)S(1)}, u32[]{:S(2)}) copy-start(f32[1,512]{1,0:T(1,128)S(1)} %get-tuple-element.61) | copy-start | bytes 6148
  140.1 8.7 %copy-start.59 = (f32[1,512]{1,0:T(1,128)}, f32[1,512]{1,0:T(1,128)S(1)}, u32[]{:S(2)}) copy-start(f32[1,512]{1,0:T(1,128)S(1)} %get-tuple-element.62) | copy-start | bytes 6148
  140.2 8.7 %copy-start.61 = (f32[1,512]{1,0:T(1,128)}, f32[1,512]{1,0:T(1,128)S(1)}, u32[]{:S(2)}) copy-start(f32[1,512]{1,0:T(1,128)S(1)} %get-tuple-element.63) | copy-start | bytes 6148
  140.2 8.7 %copy-start.63 = (f32[1,512]{1,0:T(1,128)}, f32[1,512]{1,0:T(1,128)S(1)}, u32[]{:S(2)}) copy-start(f32[1,512]{1,0:T(1,128)S(1)} %get-tuple-element.64) | copy-start | bytes 6148
  140.2 8.7 %copy-start.65 = (f32[1,512]{1,0:T(1,128)}, f32[1,512]{1,0:T(1,128)S(1)}, u32[]{:S(2)}) copy-start(f32[1,512]{1,0:T(1,128)S(1)} %get-tuple-element.65) | copy-start | bytes 6148
  149.7 7.2 %copy-start.38 = (f32[2048]{0:T(1024)}, f32[2048]{0:T(1024)S(1)}, u32[]{:S(2)}) copy-start(f32[2048]{0:T(1024)S(1)} %bitcast_rsqrt_fusion) | copy-start | bytes 24580
  157.8 4.0 copy-start.22
  157.8 35.4 %copy-start.23 = (bf16[48,32,512]{2,1,0:T(8,128)(2,1)}, bf16[48,32,512]{2,1,0:T(8,128)(2,1)S(1)}, u32[]{:S(2)}) copy-start(bf16[48,32,512]{2,1,0:T(8,128)(2,1)S(1)} %get-tuple-element.45) | copy-start | bytes 4718596
  161.8 31.4 %copy-start.17 = (bf16[2048,512]{1,0:T(8,128)(2,1)}, bf16[2048,512]{1,0:T(8,128)(2,1)S(1)}, u32[]{:S(2)}) copy-start(bf16[2048,512]{1,0:T(8,128)(2,1)S(1)} %add_convert_fusion.3) | copy-start | bytes 6291460
  161.8 31.4 %copy-start.16 = (bf16[2,1024,512]{2,1,0:T(8,128)(2,1)S(1)}, bf16[2,1024,512]{2,1,0:T(8,128)(2,1)}, u32[]{:S(2)}) copy-start(bf16[2,1024,512]{2,1,0:T(8,128)(2,1)} %param.8) | copy-start | bytes 6291460
  193.2 5.6 %copy-start.71 = (bf16[2048,1536]{1,0:T(8,128)(2,1)}, bf16[2048,1536]{1,0:T(8,128)(2,1)S(1)}, u32[]{:S(2)}) copy-start(bf16[2048,1536]{1,0:T(8,128)(2,1)S(1)} %get-tuple-element.32) | copy-start | bytes 18874372
  247.5 5.6 %copy-start.5 = (f32[2048,512]{1,0:T(8,128)}, f32[2048,512]{1,0:T(8,128)S(1)}, u32[]{:S(2)}) copy-start(f32[2048,512]{1,0:T(8,128)S(1)} %get-tuple-element.21) | copy-start | bytes 12582916
  248.2 4.9 copy-start.19
  253.1 16.6 %copy-start.4 = (f32[2048,512]{1,0:T(8,128)S(1)}, f32[2048,512]{1,0:T(8,128)}, u32[]{:S(2)}) copy-start(f32[2048,512]{1,0:T(8,128)} %bitcast_subtract_fusion) | copy-start | bytes 12582916
  253.1 16.6 %copy-start.6 = (f32[2048,512]{1,0:T(8,128)S(1)}, f32[2048,512]{1,0:T(8,128)}, u32[]{:S(2)}) copy-start(f32[2048,512]{1,0:T(8,128)} %fusion.60) | copy-start | bytes 12582916
  269.7 6.7 %copy-start.18 = (bf16[2048,512]{1,0:T(8,128)(2,1)S(1)}, bf16[2048,512]{1,0:T(8,128)(2,1)}, u32[]{:S(2)}) copy-start(bf16[2048,512]{1,0:T(8,128)(2,1)} %copy-done.17) | copy-start | bytes 6291460
  269.7 6.7 %copy-start.70 = (bf16[2048,1536]{1,0:T(8,128)(2,1)S(1)}, bf16[2048,1536]{1,0:T(8,128)(2,1)}, u32[]{:S(2)}) copy-start(bf16[2048,1536]{1,0:T(8,128)(2,1)} %get-tuple-element.90) | copy-start | bytes 18874372
  276.4 7.3 %copy-start.7 = (f32[2048,512]{1,0:T(8,128)}, f32[2048,512]{1,0:T(8,128)S(1)}, u32[]{:S(2)}) copy-start(f32[2048,512]{1,0:T(8,128)S(1)} %get-tuple-element.88) | copy-start | bytes 12582916
  276.4 5.1 copy-start.37
  276.4 5.1 copy-start.39
  291.5 8.6 %copy-start.2 = (f32[2048,512]{1,0:T(8,128)}, f32[2048,512]{1,0:T(8,128)S(1)}, u32[]{:S(2)}) copy-start(f32[2048,512]{1,0:T(8,128)S(1)} %get-tuple-element.25) | copy-start | bytes 12582916
  350.9 14.4 %copy-start.52 = (f32[4,320]{1,0:T(4,128)S(1)}, f32[4,320]{1,0:T(4,128)}, u32[]{:S(2)}) copy-start(f32[4,320]{1,0:T(4,128)} %multiply_subtract_fusion.2) | copy-start | bytes 15364
  376.4 10.4 %copy-start.45 = (f32[320]{0:T(512)S(1)}, f32[320]{0:T(512)}, u32[]{:S(2)}) copy-start(f32[320]{0:T(512)} %copy-done.44) | copy-start | bytes 3844
  376.4 10.4 %copy-start.47 = (f32[320]{0:T(512)S(1)}, f32[320]{0:T(512)}, u32[]{:S(2)}) copy-start(f32[320]{0:T(512)} %copy-done.46) | copy-start | bytes 3844
  376.4 10.4 %copy-start.49 = (f32[320]{0:T(512)S(1)}, f32[320]{0:T(512)}, u32[]{:S(2)}) copy-start(f32[320]{0:T(512)} %copy-done.48) | copy-start | bytes 3844
  376.4 10.4 %copy-start.51 = (f32[320]{0:T(512)S(1)}, f32[320]{0:T(512)}, u32[]{:S(2)}) copy-start(f32[320]{0:T(512)} %copy-done.50) | copy-start | bytes 3844
  376.4 10.3 %collective-permute-start.2 = (f32[2,3,320]{1,2,0:T(8,128)S(1)}, f32[2,3,320]{1,2,0:T(8,128)S(1)}, u32[]{:S(2)}, u32[]{:S(2)}) collective-permute-start(f32[2,3,320]{1,2,0:T(8,128)S(1)} %pad_add_fusion.1), channel_id=1, source_target_pairs={{0,1},{1,2},{2,3},{4,5},{5,6},{6,7},{8,9},{9,10},{10,11},{12,13},{... | collective-permute-start | bytes 23048 | tf_op jit(solution)/shard_map/ppermute | solution.py:47
  381.1 14.9 %collective-permute-start.4 = (f32[2,3,512]{2,1,0:T(4,128)S(1)}, f32[2,3,512]{2,1,0:T(4,128)S(1)}, u32[]{:S(2)}, u32[]{:S(2)}) collective-permute-start(f32[2,3,512]{2,1,0:T(4,128)S(1)} %get-tuple-element.49), channel_id=1, source_target_pairs={{1,0},{2,1},{3,2},{5,4},{6,5},{7,6},{9,8},{10,9},{11,10},{13,12},{... | collective-permute-start | bytes 36872 | tf_op jit(solution)/shard_map/ppermute | solution.py:39
  382.3 13.6 %collective-permute-start.5 = (f32[2,3,512]{2,1,0:T(4,128)S(1)}, f32[2,3,512]{2,1,0:T(4,128)S(1)}, u32[]{:S(2)}, u32[]{:S(2)}) collective-permute-start(f32[2,3,512]{2,1,0:T(4,128)S(1)} %get-tuple-element.50), channel_id=1, source_target_pairs={{0,1},{1,2},{2,3},{4,5},{5,6},{6,7},{8,9},{9,10},{10,11},{12,13},{... | collective-permute-start | bytes 36872 | tf_op jit(solution)/shard_map/ppermute | solution.py:36
  391.9 4.1 copy-start.54
  391.9 4.1 copy-start.56
  391.9 4.1 copy-start.58
  391.9 4.1 copy-start.60
  391.9 4.1 copy-start.62
  391.9 4.1 copy-start.64
  391.9 4.1 copy-start.66
  416.3 117.4 %copy-start.68 = (pred[27]{0:T(512)(128)(4,1)S(1)}, pred[27]{0:T(512)(128)(4,1)}, u32[]{:S(2)}) copy-start(pred[27]{0:T(512)(128)(4,1)} %get-tuple-element.18) | copy-start | bytes 85
  529.3 4.5 copy-start.12
  (22 other events, 63.2 us)
Sparse Core Ops, SparseCore 0:
  10.8 111.5 all-gather.1
  335.5 184.6 all-reduce.9
where the time goes:
time: 556 us; the launch traced here: 546 us
  other arithmetic  136 us (24%)
  local copies, waits for them, and re-layouts  133 us (24%)
  waiting for transfers between devices  130 us (23%)
  matrix products  119 us (21%)
  between operations  15.7 us (3%)
  starting transfers between devices  12.2 us (2%)
    dot_general x11, matrix products, contract(): lax.dot_general(left_side, right_side, (((left_dim,), (right_dim,)), ((),...  109 us
    psum x1, waiting for transfers between devices, local(): summed = lax.psum(grad_buckets, ('rows', 'seq'))  104 us
    another operation x3, other arithmetic  42.2 us
    concatenate x1, local copies, waits for them, and re-layouts, local(): jnp.concatenate([grad_w_in, grad_w_out, grad_w_head, vec_grads, in_rows,...  27.2 us
    all_gather x1, waiting for transfers between devices, local(): lax.all_gather(master.astype(jnp.bfloat16), 'rows', axis=0, tiled=True)  25.9 us
    add x1, other arithmetic, local(): input_grad + conv_weight[tap_index] * keep * halo_grad[:, begin:begin + f...  20.3 us
    unnamed x159, local copies, waits for them, and re-layouts  17.5 us
    reshape x1, local copies, waits for them, and re-layouts, local(): signal.reshape(rows_here, frames_here, lap_count, HOP)  14.4 us
  transfers between devices with their start and end apart: 8, of which 2 were waited for; matrix products, arithmetic and copies ran while one was open for 28% of the time, Pallas kernels for 0%

commit v1 on v0

--- a/solution.py
+++ b/solution.py
@@ -295,7 +295,7 @@
     )
     grad_buckets = jnp.pad(grad_table, ((0, NB * BR - PR), (0, 0))).reshape(NB, BR, channels)
     empty_bucket = jnp.zeros((1, BR, channels), jnp.float32)
-    summed = lax.psum(grad_buckets, ("rows", "seq"))
+    summed = lax.psum(lax.psum(grad_buckets, "seq"), "rows")
     extended = jnp.concatenate([summed, empty_bucket], axis=0)
     my_sources = lax.dynamic_slice_in_dim(source, lax.axis_index("rows") * slot_count, slot_count)
     reduced = jnp.take(extended, my_sources, axis=0)

time: 556 us -> 822 us (1.48)
  waiting for transfers between devices: 130 us -> 399 us
    psum x1 -> x2, waiting for transfers between devices: 104 us -> 372 us  [local(): summed = lax.psum(lax.psum(grad_buckets, 'seq'), 'rows')]
  transfers between devices with their start and end apart: 8 -> 9, of which waited for: 2 -> 3; matrix products, arithmetic and copies ran while one was open for 28% -> 19% of each run, Pallas kernels for 0% -> 0%
where the time goes in v1:
time: 822 us; the launch traced here: 812 us
  waiting for transfers between devices  399 us (49%)
  other arithmetic  135 us (16%)
  local copies, waits for them, and re-layouts  133 us (16%)
  matrix products  119 us (14%)
  between operations  15.3 us (2%)
  starting transfers between devices  11.6 us (1%)
    psum x2, waiting for transfers between devices, local(): summed = lax.psum(lax.psum(grad_buckets, 'seq'), 'rows')  372 us
    dot_general x11, matrix products, contract(): lax.dot_general(left_side, right_side, (((left_dim,), (right_dim,)), ((),...  109 us
    another operation x3, other arithmetic  42.2 us
    all_gather x1, waiting for transfers between devices, local(): lax.all_gather(master.astype(jnp.bfloat16), 'rows', axis=0, tiled=True)  27.2 us
    concatenate x1, local copies, waits for them, and re-layouts, local(): jnp.concatenate([grad_w_in, grad_w_out, grad_w_head, vec_grads, in_rows,...  27.2 us
    add x1, other arithmetic, local(): input_grad + conv_weight[tap_index] * keep * halo_grad[:, begin:begin + f...  20.3 us
    unnamed x159, local copies, waits for them, and re-layouts  17.9 us
  transfers between devices with their start and end apart: 9, of which 3 were waited for; matrix products, arithmetic and copies ran while one was open for 19% of the time, Pallas kernels for 0%

profile of v1, /device:TPU:0, one launch (start us, length us, event | category | flops | bytes accessed | tf_op | source)
XLA Modules:
  0.0 812.4 jit_solution(517489518048528327)
XLA Ops:
  7.2 2.5 convert_element_type.160
  10.6 2.4 collective-permute-start
  12.9 1.3 collective-permute-start.1
  15.8 2.7 reshape.271
  18.5 2.2 copy.39
  21.1 2.9 fusion.48
  24.8 1.3 collective-permute-start.3
  26.2 2.7 reshape.270
  28.9 2.2 copy.37
  32.1 2.9 fusion.47
  34.9 15.2 %multiply_convert_fusion.2 = (bf16[641,1280]{1,0:T(8,128)(2,1)}, bf16[641,1280]{1,0:T(8,128)(2,1)}) fusion(f32[641]{0:T(1024)S(1)} %fusion.74, f32[641]{0:T(1024)S(1)} %select_multiply_fusion), kind=kLoop, calls=%fused_computation.89 | loop fusion | flops 10666240 | bytes 3287048 | tf_op jit(solution)/shard_map/convert.12
  50.4 9.4 %concatenate.35 = bf16[2,1030,512]{2,1,0:T(8,128)(2,1)S(1)} concatenate(bf16[2,3,512]{2,1,0:T(4,128)(2,1)S(1)} %collective-permute-done, bf16[2,1024,512]{2,1,0:T(8,128)(2,1)} %param.8, bf16[2,3,512]{2,1,0:T(4,128)(2,1)S(1)} %collective-permute-done.1), dimensions={1} | concatenate | bytes 4218880 | tf_op jit(solution)/shard_map/concatenate | solution.py:40
  59.7 2.6 convert_element_type.164
  62.5 4.6 fusion.55
  67.1 3.2 pad_maximum_fusion.1
  70.3 10.2 %copy.40 = bf16[2,1024,4,320]{1,0,3,2:T(2,128)(2,1)} copy(bf16[2,1024,4,320]{1,3,0,2:T(8,128)(2,1)} %pad_maximum_fusion.1) | data formatting | bytes 10485760 | tf_op jit(solution)/shard_map/stack | solution.py:216
  80.5 4.9 copy.45
  85.4 9.7 %fusion.49 = f32[2048,1282]{0,1:T(8,128)} fusion(bf16[2048,1280]{0,1:T(8,128)(2,1)S(1)} %bitcast.122, bf16[641,1280]{1,0:T(8,128)(2,1)S(1)} %copy-done.20, bf16[641,1280]{1,0:T(8,128)(2,1)S(1)} %copy-done.21), kind=kOutput, calls=%fused_computation.122 | convolution fusion | flops 6727936000 | bytes 19026944 | tf_op jit(solution)/shard_map/dot_general | solution.py:104
  95.1 27.2 %all-gather.2.cloned.1.call-done = bf16[216,32,512]{2,1,0:T(8,128)(2,1)} async-done(((bf16[27,32,512]{2,1,0:T(8,128)(2,1)}), bf16[216,32,512]{2,1,0:T(8,128)(2,1)}) %all-gather.2.cloned.1.call-update) | async-done | bytes 7077904 | tf_op jit(solution)/shard_map/all_gather | solution.py:120
  122.3 10.9 %gather_fusion = bf16[137,32,512]{2,1,0:T(8,128)(2,1)} fusion(bf16[216,32,512]{2,1,0:T(8,128)(2,1)} %all-gather.2.cloned.1.call-done, s32[1024]{0:T(1024)S(1)} %pad_clamp_fusion.1), kind=kCustom, calls=%fused_computation | custom fusion | bytes 8978980 | tf_op jit(solution)/shard_map/jit(_take)/gather | solution.py:121
  133.3 4.1 bitcast_select_fusion
  137.5 2.6 broadcast_select_fusion
  140.2 2.4 slice-done
  142.7 6.1 fusion.88
  149.7 2.4 bitcast_subtract_fusion
  152.1 2.5 fusion.60
  154.6 2.3 fusion.89
  157.8 4.0 add_convert_fusion.3
  161.8 31.4 %multiply_convert_fusion = (bf16[2048,1536]{1,0:T(8,128)(2,1)S(1)}, f32[2048,1536]{1,0:T(8,128)}, f32[2048,1536]{1,0:T(8,128)}) fusion(f32[1536]{0:T(1024)S(1)} %reshape.280, bf16[2048,512]{1,0:T(8,128)(2,1)S(1)} %add_convert_fusion.3, bf16[1536,512]{1,0:T(8,128)(2,1)S(1)} %bitcast.123), kind=kOutput, calls=%fused_computation.6 | convolution fusion | flops 3428843520 | bytes 35133440 | tf_op jit(solution)/shard_map/dot_general | solution.py:104
  193.2 5.6 fusion.86
  198.8 1.9 copy-done.8
  201.6 5.8 convolution_add_fusion
  207.5 24.2 %add_convert_fusion.1 = (bf16[2048,641]{0,1:T(8,128)(2,1)S(1)}, bf16[2048,641]{0,1:T(8,128)(2,1)S(1)}, bf16[2048,641]{0,1:T(8,128)(2,1)}, bf16[2048,641]{0,1:T(8,128)(2,1)}) fusion(f32[2048,1282]{0,1:T(8,128)} %fusion.49, f32[2048,1282]{0,1:T(8,128)S(1)} %convolution_add_fusion), kind=kLoop, calls=%fused_computation.31 | loop fusion | flops 15753216 | bytes 31506432 | tf_op jit(solution)/shard_map/convert.2
  231.7 1.3 convert_reduce_fusion.1
  233.8 6.2 multiply_reduce_fusion
  240.0 4.6 fusion.52
  244.7 2.0 fusion.85
  249.5 3.6 fusion.95
  253.1 16.6 %convert_reduce_fusion = (f32[1536]{0:T(1024)S(1)}, bf16[2048,1536]{1,0:T(8,128)(2,1)}) fusion(f32[2048,1536]{1,0:T(8,128)} %get-tuple-element.33, bf16[2048,512]{1,0:T(8,128)(2,1)} %copy-done.19, bf16[1536,512]{1,0:T(8,128)(2,1)} %bitcast.126, f32[2048,1536]{1,0:T(8,128)} %get-tuple-element.84, f32[1536]{0:T(1024)S(1)} %reshape.280), kind=kOutput, calls=%fused_computation.4 | convolution fusion | flops 3274701312 | bytes 35139584 | tf_op jit(solution)/shard_map/dot_general | solution.py:104
  269.7 6.7 multiply_reduce_fusion.9
  276.4 5.1 fusion.94
  281.5 2.2 fusion.27
  283.7 1.7 fusion.59
  285.4 5.5 fusion.84
  291.5 3.2 slice-done.2
  294.7 5.3 multiply_reduce_fusion.2
  300.0 27.2 %concatenate.42 = f32[4380,512]{1,0:T(8,128)} concatenate(f32[1536,512]{1,0:T(8,128)} %fusion.94, f32[1536,512]{1,0:T(8,128)S(1)} %fusion.95, f32[1282,512]{1,0:T(8,128)} %fusion.52, f32[1,512]{1,0:T(1,128)S(1)} %bitcast.156, f32[1,512]{1,0:T(1,128)S(1)} %bitcast.155, f32[1,512]{1,0:T(1,128)S(1)} %bitcast.154, f32[1,512]{1,0:T(1,128)S(1)} %bitcast.153, f32[1,512]{1,0:T(1,128)S(1)} %bitcast.152, ...), dimensions={0} | concatenate | bytes 17940480 | tf_op jit(solution)/shard_map/concatenate | solution.py:293
  327.2 8.1 pad.35
  335.4 160.7 %all-reduce.11.cloned.1.call-done = f32[137,32,512]{2,1,0:T(8,128)} async-done(((f32[137,32,512]{2,1,0:T(8,128)}), f32[137,32,512]{2,1,0:T(8,128)}) %all-reduce.11.cloned.1.call-update) | async-done | bytes 8978448 | tf_op jit(solution)/shard_map/psum | solution.py:298
  497.9 13.5 %fusion.6 = f32[2048,1280]{0,1:T(8,128)} fusion(bf16[2048,641]{0,1:T(8,128)(2,1)} %get-tuple-element.41, bf16[2048,641]{0,1:T(8,128)(2,1)S(1)} %copy-done.15, bf16[641,1280]{1,0:T(8,128)(2,1)} %get-tuple-element.91, bf16[641,1280]{1,0:T(8,128)(2,1)} %get-tuple-element.92), kind=kOutput, calls=%fused_computation.34 | convolution fusion | flops 6738438144 | bytes 19018752 | tf_op jit(solution)/shard_map/dot_general | solution.py:104
  511.4 14.3 %reshape.268 = f32[2,1024,4,320]{1,0,3,2:T(2,128)} reshape(f32[2048,1280]{0,1:T(8,128)} %fusion.6) | data formatting | bytes 20971520 | tf_op jit(solution)/shard_map/reshape | solution.py:189
  525.7 8.5 %copy_multiply_fusion = f32[2,1024,4,320]{1,3,0,2:T(8,128)S(1)} fusion(f32[2,1024,4,320]{1,0,3,2:T(2,128)} %reshape.268, f32[4,320]{1,0:T(4,128)S(1)} %multiply_subtract_fusion.2), kind=kLoop, calls=%fused_computation.21 | loop fusion | flops 2621440 | bytes 20976640 | tf_op jit(solution)/shard_map/mul | solution.py:189
  534.5 1.8 fusion.46
  536.7 1.8 collective-permute-start.2
  538.5 2.3 pad_add_fusion
  542.9 3.4 collective-permute-start.5
  546.4 2.4 fusion.43
  548.8 2.3 copy.36
  551.2 4.1 reshape.269
  555.3 20.3 %fusion.13 = f32[2,1024,512]{2,1,0:T(8,128)} fusion(f32[2,3,512]{2,1,0:T(4,128)S(1)} %collective-permute-done.5, f32[2,3,512]{2,1,0:T(4,128)S(1)} %collective-permute-done.4, f32[2,1024,512]{2,1,0:T(8,128)} %bitcast.119, f32[2,1024,512]{2,1,0:T(8,128)} %bitcast.118, f32[512]{0:T(512)S(1)} %bitcast.135, f32[2,1024]{1,0:T(2,128)S(1)} %copy-done.31, ...), kind=kLoop, calls=%fused_computation.46 | loop fusion | flops 27262976 | bytes 12670976 | tf_op jit(solution)/shard_map/add | solution.py:279
  575.6 211.1 %all-reduce.13.cloned.1.call-done = f32[137,32,512]{2,1,0:T(8,128)} async-done(((f32[137,32,512]{2,1,0:T(8,128)}), f32[137,32,512]{2,1,0:T(8,128)}) %all-reduce.13.cloned.1.call-update) | async-done | bytes 8978448 | tf_op jit(solution)/shard_map/psum | solution.py:298
  786.7 9.1 %concatenate.43 = f32[138,32,512]{2,1,0:T(8,128)} pad(f32[137,32,512]{2,1,0:T(8,128)} %all-reduce.13.cloned.1.call-done, f32[]{:T(128)} %constant.72.clone.1), padding=0_1x0_0x0_0 | pad | bytes 18022404 | tf_op jit(solution)/shard_map/concatenate | solution.py:299
  795.8 4.4 gather_fusion.1
  800.2 5.5 multiply_subtract_fusion
  (223 shorter events, 16.3 us)
Async XLA Ops:
  7.2 115.1 %all-gather.2.cloned.1.call-start = ((), (), s32[]{:S(2)}) async-start(), calls=%async_computation | async-start | bytes 7962624 | tf_op jit(solution)/shard_map/all_gather | solution.py:120
  9.8 486.3 %all-reduce.11.cloned.1.call-start = ((), (), s32[]{:S(2)}) async-start(), calls=%async_computation.1 | async-start | bytes 17956864 | tf_op jit(solution)/shard_map/psum | solution.py:298
  10.6 39.8 %collective-permute-start = (bf16[2,3,512]{2,1,0:T(4,128)(2,1)S(1)}, bf16[2,3,512]{2,1,0:T(4,128)(2,1)S(1)}, u32[]{:S(2)}, u32[]{:S(2)}) collective-permute-start(bf16[2,3,512]{2,1,0:T(4,128)(2,1)S(1)} %get-tuple-element.55), channel_id=1, source_target_pairs={{0,1},{1,2},{2,3},{4,5},{5,6},{6,7},{8,9},{9,10},{10,11},{12,13},{... | collective-permute-start | bytes 18440 | tf_op jit(solution)/shard_map/ppermute | solution.py:36
  12.9 37.4 %collective-permute-start.1 = (bf16[2,3,512]{2,1,0:T(4,128)(2,1)S(1)}, bf16[2,3,512]{2,1,0:T(4,128)(2,1)S(1)}, u32[]{:S(2)}, u32[]{:S(2)}) collective-permute-start(bf16[2,3,512]{2,1,0:T(4,128)(2,1)S(1)} %get-tuple-element.54), channel_id=1, source_target_pairs={{1,0},{2,1},{3,2},{5,4},{6,5},{7,6},{9,8},{10,9},{11,10},{13,12},{... | collective-permute-start | bytes 18440 | tf_op jit(solution)/shard_map/ppermute | solution.py:39
  20.9 11.2 %copy-start.44 = (f32[320]{0:T(512)}, f32[320]{0:T(512)S(1)}, u32[]{:S(2)}) copy-start(f32[320]{0:T(512)S(1)} %get-tuple-element.75) | copy-start | bytes 3844
  20.9 11.2 %copy-start.46 = (f32[320]{0:T(512)}, f32[320]{0:T(512)S(1)}, u32[]{:S(2)}) copy-start(f32[320]{0:T(512)S(1)} %get-tuple-element.76) | copy-start | bytes 3844
  20.9 11.2 %copy-start.48 = (f32[320]{0:T(512)}, f32[320]{0:T(512)S(1)}, u32[]{:S(2)}) copy-start(f32[320]{0:T(512)S(1)} %get-tuple-element.77) | copy-start | bytes 3844
  20.9 11.2 %copy-start.50 = (f32[320]{0:T(512)}, f32[320]{0:T(512)S(1)}, u32[]{:S(2)}) copy-start(f32[320]{0:T(512)S(1)} %get-tuple-element.78) | copy-start | bytes 3844
  21.1 119.1 %copy-start.24 = (f32[2,1024]{1,0:T(2,128)}, f32[2,1024]{1,0:T(2,128)S(1)}, u32[]{:S(2)}) copy-start(f32[2,1024]{1,0:T(2,128)S(1)} %get-tuple-element.68) | copy-start | bytes 24580
  21.1 119.1 %copy-start.26 = (f32[2,1024]{1,0:T(2,128)}, f32[2,1024]{1,0:T(2,128)S(1)}, u32[]{:S(2)}) copy-start(f32[2,1024]{1,0:T(2,128)S(1)} %get-tuple-element.72) | copy-start | bytes 24580
  21.1 119.1 %copy-start.28 = (f32[2,1024]{1,0:T(2,128)}, f32[2,1024]{1,0:T(2,128)S(1)}, u32[]{:S(2)}) copy-start(f32[2,1024]{1,0:T(2,128)S(1)} %get-tuple-element.73) | copy-start | bytes 24580
  21.1 119.1 %copy-start.30 = (f32[2,1024]{1,0:T(2,128)}, f32[2,1024]{1,0:T(2,128)S(1)}, u32[]{:S(2)}) copy-start(f32[2,1024]{1,0:T(2,128)S(1)} %get-tuple-element.69) | copy-start | bytes 24580
  21.1 119.1 %copy-start.32 = (f32[2,1024]{1,0:T(2,128)}, f32[2,1024]{1,0:T(2,128)S(1)}, u32[]{:S(2)}) copy-start(f32[2,1024]{1,0:T(2,128)S(1)} %get-tuple-element.70) | copy-start | bytes 24580
  21.1 119.1 %copy-start.34 = (f32[2,1024]{1,0:T(2,128)}, f32[2,1024]{1,0:T(2,128)S(1)}, u32[]{:S(2)}) copy-start(f32[2,1024]{1,0:T(2,128)S(1)} %get-tuple-element.71) | copy-start | bytes 24580
  24.8 37.5 %collective-permute-start.3 = (f32[2,3,320]{1,2,0:T(8,128)}, f32[2,3,320]{1,2,0:T(8,128)}, u32[]{:S(2)}, u32[]{:S(2)}) collective-permute-start(f32[2,3,320]{1,2,0:T(8,128)} %slice.387), channel_id=1, source_target_pairs={{1,0},{2,1},{3,2},{5,4},{6,5},{7,6},{9,8},{10,9},{11,10},{13,12},{... | collective-permute-start | bytes 23048 | tf_op jit(solution)/shard_map/ppermute | solution.py:47
  26.2 5.0 copy-start.69
  26.2 5.1 copy-start.66
  50.3 106.6 %copy-start.36 = (s32[1,8,2,128]{3,1,2,0:T(8,128)}, s32[1,8,2,128]{3,1,2,0:T(8,128)S(1)}, u32[]{:S(2)}) copy-start(s32[1,8,2,128]{3,1,2,0:T(8,128)S(1)} %copy.53) | copy-start | bytes 24580
  80.5 4.9 copy-start.20
  80.5 4.9 copy-start.21
  133.3 4.2 copy-start.1
  137.4 14.7 %copy-start.13 = (bf16[4384,512]{1,0:T(8,128)(2,1)}, bf16[4384,512]{1,0:T(8,128)(2,1)S(1)}, u32[]{:S(2)}) copy-start(bf16[4384,512]{1,0:T(8,128)(2,1)S(1)} %bitcast_select_fusion) | copy-start | bytes 13467652
  137.4 5.3 slice-start
  137.5 5.2 slice-start.1
  140.1 8.7 %copy-start.52 = (f32[1,512]{1,0:T(1,128)}, f32[1,512]{1,0:T(1,128)S(1)}, u32[]{:S(2)}) copy-start(f32[1,512]{1,0:T(1,128)S(1)} %get-tuple-element.59) | copy-start | bytes 6148
  140.1 8.7 %copy-start.54 = (f32[1,512]{1,0:T(1,128)}, f32[1,512]{1,0:T(1,128)S(1)}, u32[]{:S(2)}) copy-start(f32[1,512]{1,0:T(1,128)S(1)} %get-tuple-element.60) | copy-start | bytes 6148
  140.1 8.7 %copy-start.56 = (f32[1,512]{1,0:T(1,128)}, f32[1,512]{1,0:T(1,128)S(1)}, u32[]{:S(2)}) copy-start(f32[1,512]{1,0:T(1,128)S(1)} %get-tuple-element.61) | copy-start | bytes 6148
  140.1 8.7 %copy-start.58 = (f32[1,512]{1,0:T(1,128)}, f32[1,512]{1,0:T(1,128)S(1)}, u32[]{:S(2)}) copy-start(f32[1,512]{1,0:T(1,128)S(1)} %get-tuple-element.62) | copy-start | bytes 6148
  140.1 8.7 %copy-start.60 = (f32[1,512]{1,0:T(1,128)}, f32[1,512]{1,0:T(1,128)S(1)}, u32[]{:S(2)}) copy-start(f32[1,512]{1,0:T(1,128)S(1)} %get-tuple-element.63) | copy-start | bytes 6148
  140.1 8.7 %copy-start.62 = (f32[1,512]{1,0:T(1,128)}, f32[1,512]{1,0:T(1,128)S(1)}, u32[]{:S(2)}) copy-start(f32[1,512]{1,0:T(1,128)S(1)} %get-tuple-element.64) | copy-start | bytes 6148
  140.2 8.7 %copy-start.64 = (f32[1,512]{1,0:T(1,128)}, f32[1,512]{1,0:T(1,128)S(1)}, u32[]{:S(2)}) copy-start(f32[1,512]{1,0:T(1,128)S(1)} %get-tuple-element.65) | copy-start | bytes 6148
  149.7 7.2 copy-start.38
  157.8 4.0 copy-start.22
  157.8 35.4 %copy-start.23 = (bf16[48,32,512]{2,1,0:T(8,128)(2,1)}, bf16[48,32,512]{2,1,0:T(8,128)(2,1)S(1)}, u32[]{:S(2)}) copy-start(bf16[48,32,512]{2,1,0:T(8,128)(2,1)S(1)} %get-tuple-element.45) | copy-start | bytes 4718596
  161.8 31.4 %copy-start.17 = (bf16[2048,512]{1,0:T(8,128)(2,1)}, bf16[2048,512]{1,0:T(8,128)(2,1)S(1)}, u32[]{:S(2)}) copy-start(bf16[2048,512]{1,0:T(8,128)(2,1)S(1)} %add_convert_fusion.3) | copy-start | bytes 6291460
  161.8 31.4 %copy-start.16 = (bf16[2,1024,512]{2,1,0:T(8,128)(2,1)S(1)}, bf16[2,1024,512]{2,1,0:T(8,128)(2,1)}, u32[]{:S(2)}) copy-start(bf16[2,1024,512]{2,1,0:T(8,128)(2,1)} %param.8) | copy-start | bytes 6291460
  193.2 5.6 copy-start.71
  247.5 5.6 copy-start.5
  248.2 4.9 copy-start.19
  253.1 16.6 %copy-start.4 = (f32[2048,512]{1,0:T(8,128)S(1)}, f32[2048,512]{1,0:T(8,128)}, u32[]{:S(2)}) copy-start(f32[2048,512]{1,0:T(8,128)} %bitcast_subtract_fusion) | copy-start | bytes 12582916
  253.1 16.6 %copy-start.6 = (f32[2048,512]{1,0:T(8,128)S(1)}, f32[2048,512]{1,0:T(8,128)}, u32[]{:S(2)}) copy-start(f32[2048,512]{1,0:T(8,128)} %fusion.60) | copy-start | bytes 12582916
  269.6 6.7 copy-start.18
  269.7 6.7 copy-start.70
  276.4 7.3 copy-start.7
  276.4 5.1 copy-start.37
  276.4 5.1 copy-start.39
  291.0 3.7 slice-start.2
  291.5 8.6 %copy-start.2 = (f32[2048,512]{1,0:T(8,128)}, f32[2048,512]{1,0:T(8,128)S(1)}, u32[]{:S(2)}) copy-start(f32[2048,512]{1,0:T(8,128)S(1)} %get-tuple-element.25) | copy-start | bytes 12582916
  335.3 451.3 %all-reduce.13.cloned.1.call-start = ((), (), s32[]{:S(2)}) async-start(), calls=%async_computation.2 | async-start | bytes 17956864 | tf_op jit(solution)/shard_map/psum | solution.py:298
  536.7 9.7 %copy-start.45 = (f32[320]{0:T(512)S(1)}, f32[320]{0:T(512)}, u32[]{:S(2)}) copy-start(f32[320]{0:T(512)} %copy-done.44) | copy-start | bytes 3844
  536.7 9.7 %copy-start.47 = (f32[320]{0:T(512)S(1)}, f32[320]{0:T(512)}, u32[]{:S(2)}) copy-start(f32[320]{0:T(512)} %copy-done.46) | copy-start | bytes 3844
  536.7 9.7 %copy-start.49 = (f32[320]{0:T(512)S(1)}, f32[320]{0:T(512)}, u32[]{:S(2)}) copy-start(f32[320]{0:T(512)} %copy-done.48) | copy-start | bytes 3844
  536.7 9.7 %copy-start.51 = (f32[320]{0:T(512)S(1)}, f32[320]{0:T(512)}, u32[]{:S(2)}) copy-start(f32[320]{0:T(512)} %copy-done.50) | copy-start | bytes 3844
  536.7 9.7 %collective-permute-start.2 = (f32[2,3,320]{1,2,0:T(8,128)S(1)}, f32[2,3,320]{1,2,0:T(8,128)S(1)}, u32[]{:S(2)}, u32[]{:S(2)}) collective-permute-start(f32[2,3,320]{1,2,0:T(8,128)S(1)} %pad_add_fusion.1), channel_id=1, source_target_pairs={{0,1},{1,2},{2,3},{4,5},{5,6},{6,7},{8,9},{9,10},{10,11},{12,13},{... | collective-permute-start | bytes 23048 | tf_op jit(solution)/shard_map/ppermute | solution.py:47
  541.6 13.6 %collective-permute-start.4 = (f32[2,3,512]{2,1,0:T(4,128)S(1)}, f32[2,3,512]{2,1,0:T(4,128)S(1)}, u32[]{:S(2)}, u32[]{:S(2)}) collective-permute-start(f32[2,3,512]{2,1,0:T(4,128)S(1)} %get-tuple-element.49), channel_id=1, source_target_pairs={{1,0},{2,1},{3,2},{5,4},{6,5},{7,6},{9,8},{10,9},{11,10},{13,12},{... | collective-permute-start | bytes 36872 | tf_op jit(solution)/shard_map/ppermute | solution.py:39
  542.9 12.3 %collective-permute-start.5 = (f32[2,3,512]{2,1,0:T(4,128)S(1)}, f32[2,3,512]{2,1,0:T(4,128)S(1)}, u32[]{:S(2)}, u32[]{:S(2)}) collective-permute-start(f32[2,3,512]{2,1,0:T(4,128)S(1)} %get-tuple-element.50), channel_id=1, source_target_pairs={{0,1},{1,2},{2,3},{4,5},{5,6},{6,7},{8,9},{9,10},{10,11},{12,13},{... | collective-permute-start | bytes 36872 | tf_op jit(solution)/shard_map/ppermute | solution.py:36
  551.1 4.1 copy-start.53
  551.1 4.1 copy-start.55
  551.1 4.1 copy-start.57
  551.2 4.1 copy-start.59
  551.2 4.1 copy-start.61
  551.2 4.1 copy-start.63
  551.2 4.1 copy-start.65
  795.8 4.4 copy-start.12
  (23 other events, 60.9 us)
Sparse Core Ops, SparseCore 0:
  10.8 111.4 all-gather.1
  335.5 160.5 all-reduce.10
  500.0 286.6 all-reduce.12
